TPU v7x, 512 devices: a whole 4x8x8 slice. The times are simulated.
512 devices in a mesh: ka: 8 (over z_lo, core), pair: 64 (over y, z_hi, x).
Axes of the slice: x: 4, y: 8, z: 8 (z_hi: 2, z_lo: 4; z = z_hi * 4 + z_lo), core: 2. Of those that a mesh axis runs over, the one named last changes fastest.
Arguments:
- cond_orbitals: bfloat16 [8, 2048, 8192], P('ka', 'pair'), may hold values from -6 to 6
- cond_energy: float32 [8, 8192], P('ka', 'pair'), may hold values from 0.5 to 8
- val_orbitals: bfloat16 [512, 2048], P(('ka', 'pair')), may hold values from -6 to 6
- val_energy: bfloat16 [512], P(('ka', 'pair')), may hold values from -8 to -0.5
- val_slots: int32 [8, 64, 16], P('ka', 'pair'), may hold values from 0 to 511
- owner_count: int32 [8, 64], P('ka', 'pair'), may hold values from 1 to 16, as said below
Outputs:
- response: float32 [8, 2048, 512], P('ka', 'pair')
Inputs may be any that keep to these rules, and one draw needn't show every extreme that they name: `owner_count`: in every lane some owner has exactly 16 live slots.
All inputs are finite; a program needn't handle non-finite values.
Results may differ from a plain program's by a relative error of at most 0.0047.
The roundings to bfloat16 on the way count: a program that leaves them out, or rounds other values in their place, can miss the bound.
Values may be sent and summed in bfloat16 or wider, within the bound.
No kernel may reach another device: no remote copies, remote signals or barrier semaphores. Data moves between devices by JAX's collectives and lax.ppermute only.
A program may use at most 64 MiB of HBM per device.

v0:
```python
import jax
import jax.numpy as jnp
from jax import lax
from jax.sharding import PartitionSpec as P

BC = 128
GA = 16
GB = 128
WIN = 512
SLOTS = 16


def cosine_table(length):
    freq = lax.iota(jnp.float32, length)[:, None]
    point = lax.iota(jnp.float32, length)[None, :]
    factor = jnp.where(freq == 0, jnp.sqrt(1.0 / length), jnp.sqrt(2.0 / length))
    return (factor * jnp.cos(jnp.pi * (point + 0.5) * freq / length)).astype(jnp.bfloat16)


def owner_terms(picked, e_pick, live, cond_block, e_cond, table_a, table_b):
    slots = picked.shape[0]
    pair_real = (
        picked[:, None, :].astype(jnp.float32) * cond_block[None].astype(jnp.float32)
    ).astype(jnp.bfloat16)
    count = slots * cond_block.shape[0]
    rows = pair_real.reshape(count * GA, GB)
    first = jnp.dot(rows, table_b.T, preferred_element_type=jnp.float32).astype(jnp.bfloat16)
    first = first.reshape(count, GA, GB)
    moved = jnp.einsum("ja,pak->pjk", table_a, first, preferred_element_type=jnp.float32)
    moved = moved.astype(jnp.bfloat16).reshape(count, GA * GB)
    weight = live[:, None] * 2.0 / (e_cond[None, :] - e_pick[:, None])
    weighted = (moved[:, :WIN].astype(jnp.float32) * weight.reshape(count, 1)).astype(jnp.bfloat16)
    return (moved, weighted)


def shards(cond_orbitals, cond_energy, val_orbitals, val_energy, val_slots, owner_count):
    cond_block = lax.all_to_all(cond_orbitals, "pair", split_axis=2, concat_axis=1, tiled=True)[0].T
    all_orb, all_energy = (
        lax.all_gather(val_orbitals, ("ka", "pair"), axis=0, tiled=True),
        lax.all_gather(val_energy, ("ka", "pair"), axis=0, tiled=True),
    )
    slots = val_slots[0, 0]
    picked = jnp.take(all_orb, slots, axis=0)
    e_pick = jnp.take(all_energy, slots).astype(jnp.float32)
    live = (lax.iota(jnp.int32, slots.shape[0]) < owner_count[0, 0]).astype(jnp.float32)
    moved, weighted = owner_terms(
        picked, e_pick, live, cond_block, cond_energy[0], cosine_table(GA), cosine_table(GB)
    )
    owners = lax.axis_size("pair")
    grid_len = moved.shape[1]
    own_rows = grid_len // owners
    summed = lax.psum(
        lax.dot_general(
            moved, weighted, (((0,), (0,)), ((), ())), preferred_element_type=jnp.float32
        ),
        "pair",
    )
    mine = lax.dynamic_slice_in_dim(summed, lax.axis_index("pair") * own_rows, own_rows, 0)
    scale = 2.0 / (SLOTS * BC * owners)
    return (mine * scale)[None]


def solution(mesh):
    return jax.shard_map(
        shards,
        mesh=mesh,
        in_specs=(
            P("ka", "pair", None),
            P("ka", "pair"),
            P(("ka", "pair"), None),
            P(("ka", "pair")),
            P("ka", "pair", None),
            P("ka", "pair"),
        ),
        out_specs=P("ka", "pair", None),
        check_vma=False,
    )
```

profile of v0, /device:TPU:2, one launch (start us, length us, event | category | flops | bytes accessed | tf_op | source)
XLA Modules:
  0.0 2326.5 jit_solution(4205094719186806137)
XLA Ops:
  6.5 0.7 all-gather.3.cloned.1.call-update
  7.3 8.6 copy.18
  15.9 0.5 broadcast.173
  16.4 45.2 %reduce = bf16[8192,32]{1,0:T(8,128)(2,1)S(1)} reduce(bf16[8192,1,32]{2,1,0:T(2,128)(2,1)} %bitcast.45, bf16[]{:T(256)} %broadcast.173), dimensions={1}, to_apply=%bitcast.34.reduce_sub_computation | reduce | bytes 1048578
  61.6 2.8 reshape.162
  64.4 19.1 all-to-all-start
  85.0 103.8 %all-reduce = bf16[512]{0:T(512)(128)(2,1)S(1)} all-reduce(bf16[512]{0:T(512)(128)(2,1)S(1)} %dynamic-update-slice), channel_id=1, replica_groups=mesh['ka'=8,'pair'=64] {'ka','pair'}, use_global_device_ids=true, to_apply=%add | all-reduce | flops 512 | bytes 2048
  188.8 0.7 gather_fusion.1
  189.6 7.2 reshape.163
  196.8 8.0 copy.19
  204.9 0.2 copy.23
  205.1 0.6 copy.20
  205.7 0.3 copy.21
  206.0 1193.1 %all-gather.3.cloned.1.call-done = bf16[512,1,2048]{2,1,0:T(2,128)(2,1)} async-done(((bf16[1,1,2048]{2,1,0:T(2,128)(2,1)}), bf16[512,1,2048]{2,1,0:T(2,128)(2,1)}) %all-gather.3.cloned.1.call-update) | async-done | bytes 2097168 | tf_op jit(solution)/shard_map/all_gather | solution.py:39
  1399.1 3.5 copy.28
  1402.6 0.6 gather_fusion
  1403.3 5.4 multiply_convert_fusion
  1408.6 13.5 convert_element_type.68
  1422.1 5.9 convolution_convert_fusion
  1428.0 5.6 convolution_convert_fusion.1
  1433.7 10.9 copy.27
  1444.5 10.6 fusion
  1455.1 863.1 %all-reduce.3.cloned.1.call-done = f32[2048,512]{1,0:T(8,128)} async-done(((f32[2048,512]{1,0:T(8,128)}), f32[2048,512]{1,0:T(8,128)}) %all-reduce.3.cloned.1.call-update) | async-done | bytes 4194320 | tf_op jit(solution)/shard_map/psum | solution.py:52
  2318.2 1.5 multiply_bitcast_fusion
  (19 shorter events, 0.5 us)
Async XLA Ops:
  6.5 182.2 %copy-start.1 = (s32[1,1,16]{2,1,0:T(1,128)S(1)}, s32[1,1,16]{2,1,0:T(1,128)}, u32[]{:S(2)}) copy-start(s32[1,1,16]{2,1,0:T(1,128)} %param.10) | copy-start | bytes 196
  6.5 183.0 %copy-start = (f32[1,128]{1,0:T(1,128)S(1)}, f32[1,128]{1,0:T(1,128)}, u32[]{:S(2)}) copy-start(f32[1,128]{1,0:T(1,128)} %param.7) | copy-start | bytes 1540
  6.5 1392.6 %all-gather.3.cloned.1.call-start = ((), (), s32[]{:S(2)}) async-start(), calls=%async_computation.2 | async-start | bytes 4202496 | tf_op jit(solution)/shard_map/all_gather | solution.py:39
  64.4 125.2 %all-to-all-start = ((bf16[64,2,2048]{2,1,0:T(2,128)(2,1)}), bf16[64,2,2048]{2,1,0:T(2,128)(2,1)S(1)}, u32[]{:S(2)}, u32[]{:S(2)}) async-start(bf16[64,2,2048]{2,1,0:T(2,128)(2,1)} %reshape.162), calls=%async_computation | async-start | bytes 1048576 | tf_op jit(solution)/shard_map/all_to_all | solution.py:37
  83.5 2234.7 %all-reduce.3.cloned.1.call-start = ((), (), s32[]{:S(2)}) async-start(), calls=%async_computation.1 | async-start | bytes 8388608 | tf_op jit(solution)/shard_map/psum | solution.py:52
Sparse Core Ops, SparseCore 0:
  9.6 1389.4 all-gather.2
  1455.2 862.9 all-reduce.2
where the time goes:
time: 2330 us
  waiting for transfers between devices  2060 us (88%)
  blocking collectives  104 us (4%)
  local copies, waits for them, and re-layouts  57.4 us (2%)
  other arithmetic  52.3 us (2%)
    all_gather x1, waiting for transfers between devices, shards(): lax.all_gather(val_orbitals, ('ka', 'pair'), axis=0, tiled=True)  1190 us
    psum x1, waiting for transfers between devices, shards(): lax.psum(lax.dot_general(moved, weighted, (((0,), (0,)), ((), ())), prefe...  863 us
    unnamed x1, blocking collectives  104 us
  transfers between devices with their start and end apart: 3, of which 2 were waited for; matrix products, arithmetic and copies ran while one was open for 3% of the time, Pallas kernels for 0%

commit v1 on v0

--- a/solution.py
+++ b/solution.py
@@ -8,6 +8,13 @@
 GB = 128
 WIN = 512
 SLOTS = 16
+
+
+def match_the_state(shard_in, pos_dim):
+    finding = jax.lax.all_to_all(
+        jnp.stack([shard_in] * jax.lax.axis_size(("ka", "pair")), axis=0), ("ka", "pair"), 0, 0
+    )
+    return jnp.concatenate(finding, pos_dim)
 
 
 def cosine_table(length):
@@ -36,7 +43,7 @@
 def shards(cond_orbitals, cond_energy, val_orbitals, val_energy, val_slots, owner_count):
     cond_block = lax.all_to_all(cond_orbitals, "pair", split_axis=2, concat_axis=1, tiled=True)[0].T
     all_orb, all_energy = (
-        lax.all_gather(val_orbitals, ("ka", "pair"), axis=0, tiled=True),
+        match_the_state(val_orbitals, 0),
         lax.all_gather(val_energy, ("ka", "pair"), axis=0, tiled=True),
     )
     slots = val_slots[0, 0]

time: 2330 us -> 1200 us (0.52)
  waiting for transfers between devices: 2060 us -> 854 us
  blocking collectives: 104 us -> 136 us
    all_gather x1 -> x0, waiting for transfers between devices: 1190 us -> none  [shards(): lax.all_gather(val_orbitals, ('ka', 'pair'), axis=0, tiled=True)]
    unnamed x1, blocking collectives: 104 us -> 136 us
  transfers between devices with their start and end apart: 3 -> 3, of which waited for: 2 -> 1; matrix products, arithmetic and copies ran while one was open for 3% -> 3% of each run, Pallas kernels for 0% -> 0%
where the time goes in v1:
time: 1200 us
  waiting for transfers between devices  854 us (71%)
  blocking collectives  136 us (11%)
  local copies, waits for them, and re-layouts  73 us (6%)
  other arithmetic  65.5 us (5%)
  starting transfers between devices  36.3 us (3%)
  matrix products  22.1 us (2%)
  between operations  14.8 us (1%)
    psum x1, waiting for transfers between devices, shards(): lax.psum(lax.dot_general(moved, weighted, (((0,), (0,)), ((), ())), prefe...  854 us
    unnamed x1, blocking collectives  136 us
    unnamed x3, other arithmetic  45.3 us
    unnamed x17, local copies, waits for them, and re-layouts  43 us
  transfers between devices with their start and end apart: 3, of which 1 were waited for; matrix products, arithmetic and copies ran while one was open for 3% of the time, Pallas kernels for 0%

profile of v1, /device:TPU:2, one launch (start us, length us, event | category | flops | bytes accessed | tf_op | source)
XLA Modules:
  0.0 1201.9 jit_solution(8501460629408461598)
XLA Ops:
  6.5 8.6 copy.18
  15.7 45.2 %reduce.1 = bf16[8192,32]{1,0:T(8,128)(2,1)S(1)} reduce(bf16[8192,1,32]{2,1,0:T(2,128)(2,1)} %bitcast.44, bf16[]{:T(256)} %broadcast.177), dimensions={1}, to_apply=%bitcast.33.reduce_sub_computation | reduce | bytes 1048578
  60.9 2.8 reshape.168
  63.6 19.1 %all-to-all-start.1 = ((bf16[64,2,2048]{2,1,0:T(2,128)(2,1)}), bf16[64,2,2048]{2,1,0:T(2,128)(2,1)S(1)}, u32[]{:S(2)}, u32[]{:S(2)}) async-start(bf16[64,2,2048]{2,1,0:T(2,128)(2,1)} %reshape.168), calls=%async_computation.1 | async-start | bytes 1048576 | tf_op jit(solution)/shard_map/all_to_all | solution.py:44
  82.8 4.1 stack.2
  86.9 13.2 %reduce.2 = bf16[512,2048]{1,0:T(8,128)(2,1)S(1)} reduce(bf16[512,1,2048]{2,1,0:T(2,128)(2,1)} %stack.2, bf16[]{:T(256)} %broadcast.177), dimensions={1}, to_apply=%stack.2.reduce_sub_computation | reduce | bytes 4194306 | tf_op jit(solution)/shard_map/stack | solution.py:15
  100.1 2.8 reshape.170
  102.9 17.2 %all-to-all-start = ((bf16[512,2,1024]{2,1,0:T(2,128)(2,1)}), bf16[512,2,1024]{2,1,0:T(2,128)(2,1)S(1)}, u32[]{:S(2)}, u32[]{:S(2)}) async-start(bf16[512,2,1024]{2,1,0:T(2,128)(2,1)} %reshape.170), calls=%async_computation | async-start | bytes 4194304 | tf_op jit(solution)/shard_map/all_to_all | solution.py:14
  121.6 136.1 %all-reduce = bf16[512]{0:T(512)(128)(2,1)S(1)} all-reduce(bf16[512]{0:T(512)(128)(2,1)S(1)} %dynamic-update-slice), channel_id=1, replica_groups=mesh['ka'=8,'pair'=64] {'ka','pair'}, use_global_device_ids=true, to_apply=%add | all-reduce | flops 512 | bytes 2048
  257.7 0.7 gather_fusion.1
  258.5 7.1 reshape.169
  265.6 8.0 copy.19
  273.8 1.6 copy.20
  275.4 1.6 copy.21
  277.0 6.6 reshape.171
  283.6 3.5 copy.28
  287.8 5.4 multiply_convert_fusion
  293.1 13.5 %convert_element_type.68 = bf16[32768,128]{1,0:T(8,128)(2,1)} reshape(bf16[16,128,2048]{2,1,0:T(8,128)(2,1)} %multiply_convert_fusion) | data formatting | bytes 16777216 | tf_op jit(solution)/shard_map/convert_element_type | solution.py:31
  306.6 5.9 convolution_convert_fusion
  312.5 5.6 convolution_convert_fusion.1
  318.1 10.9 copy.27
  329.0 10.6 fusion
  339.6 854.0 %all-reduce.3.cloned.1.call-done = f32[2048,512]{1,0:T(8,128)} async-done(((f32[2048,512]{1,0:T(8,128)}), f32[2048,512]{1,0:T(8,128)}) %all-reduce.3.cloned.1.call-update) | async-done | bytes 4194320 | tf_op jit(solution)/shard_map/psum | solution.py:59
  1193.6 1.5 multiply_bitcast_fusion
  (25 shorter events, 1.8 us)
Async XLA Ops:
  6.5 76.2 %copy-start = (bf16[1,2048]{1,0:T(2,128)(2,1)S(1)}, bf16[1,2048]{1,0:T(2,128)(2,1)}, u32[]{:S(2)}) copy-start(bf16[1,2048]{1,0:T(2,128)(2,1)} %param.8) | copy-start | bytes 12292
  63.6 39.3 %all-to-all-start.1 = ((bf16[64,2,2048]{2,1,0:T(2,128)(2,1)}), bf16[64,2,2048]{2,1,0:T(2,128)(2,1)S(1)}, u32[]{:S(2)}, u32[]{:S(2)}) async-start(bf16[64,2,2048]{2,1,0:T(2,128)(2,1)} %reshape.168), calls=%async_computation.1 | async-start | bytes 1048576 | tf_op jit(solution)/shard_map/all_to_all | solution.py:44
  86.9 170.8 %copy-start.2 = (s32[1,1,16]{2,1,0:T(1,128)S(1)}, s32[1,1,16]{2,1,0:T(1,128)}, u32[]{:S(2)}) copy-start(s32[1,1,16]{2,1,0:T(1,128)} %param.10) | copy-start | bytes 196
  86.9 171.5 %copy-start.1 = (f32[1,128]{1,0:T(1,128)S(1)}, f32[1,128]{1,0:T(1,128)}, u32[]{:S(2)}) copy-start(f32[1,128]{1,0:T(1,128)} %param.7) | copy-start | bytes 1540
  102.9 174.1 %all-to-all-start = ((bf16[512,2,1024]{2,1,0:T(2,128)(2,1)}), bf16[512,2,1024]{2,1,0:T(2,128)(2,1)S(1)}, u32[]{:S(2)}, u32[]{:S(2)}) async-start(bf16[512,2,1024]{2,1,0:T(2,128)(2,1)} %reshape.170), calls=%async_computation | async-start | bytes 4194304 | tf_op jit(solution)/shard_map/all_to_all | solution.py:14
  120.1 1073.5 %all-reduce.3.cloned.1.call-start = ((), (), s32[]{:S(2)}) async-start(), calls=%async_computation.2 | async-start | bytes 8388608 | tf_op jit(solution)/shard_map/psum | solution.py:59
Sparse Core Ops, SparseCore 0:
  339.8 853.8 all-reduce.2
